TPU v7x, 32 devices: a whole 2x2x4 slice. The times are simulated.
32 devices in a mesh: space: 8 (over y, x, core), band: 4 (over z).
Axes of the slice: x: 2, y: 2, z: 4, core: 2. Of those that a mesh axis runs over, the one named last changes fastest.
Arguments:
- vectors: float32 [32768, 1024], P('space', 'band')
- blocks: float32 [128, 7, 256, 256], P('space'), may hold values from -0.125 to 0.125
- neighbours: int32 [128, 7], P('space'), may hold values from 0 to 127, as said below
Outputs:
- rotated: float32 [32768, 1024], P('space', 'band')
Inputs may be any that keep to these rules, and one draw needn't show every extreme that they name: neighbours[e, k] lies within 2 places of e in the cyclic order of the elements; for every e, neighbours[e, 1] = e - 2 and neighbours[e, 2] = e + 2, taken modulo 128.
All inputs are finite; a program needn't handle non-finite values.
Results may differ from a plain program's by a relative error of at most 0.000098.
Values sent between devices are 32-bit elements; how exact they have to be, the bound alone decides.
A program may use at most 128 MiB of HBM per device.

v0:
```python
import jax
import jax.numpy as jnp
from jax import lax
from jax.sharding import PartitionSpec as P

VECTORS = 1024
REACH = 2


def padded_2(x, sides, width):
    for axis, dim in sides:
        size, length = (lax.axis_size(axis), x.shape[dim])
        up = [(i, (i + 1) % size) for i in range(size)]
        down = [(j, i) for i, j in up]
        last = lax.slice_in_dim(x, length - width, length, axis=dim)
        first = lax.slice_in_dim(x, 0, width, axis=dim)
        before = lax.ppermute(last, axis, up)
        after = lax.ppermute(first, axis, down)
        x = jnp.concatenate([before, x, after], axis=dim)
    return x


def per_device(vectors, blocks, neighbours):
    elem_dev = blocks.shape[0]
    basis = blocks.shape[2]
    panel = vectors.shape[1]
    space_count = lax.axis_size("space")
    total_elements = elem_dev * space_count
    order = total_elements * basis
    first_id = lax.axis_index("space") * elem_dev
    local_ids = jnp.arange(elem_dev, dtype=jnp.int32)
    global_ids = first_id + local_ids
    offsets = (neighbours - global_ids[:, None] + REACH + total_elements) % total_elements - REACH
    slots = local_ids[:, None] + REACH + offsets

    def apply_operator(field):
        padded = padded_2(field, (("space", 0),), REACH * basis)
        padded = padded.reshape(elem_dev + 2 * REACH, basis, panel)
        picked = padded[slots]
        result = jnp.einsum("lkij,lkjm->lim", blocks, picked, precision=lax.Precision.HIGHEST)
        return result.reshape(elem_dev * basis, panel)

    first_step = (apply_operator(vectors) - 0.5 * vectors) / 1.5
    filtered = 2.0 * (apply_operator(first_step) - 0.5 * first_step) / 1.5 - vectors
    row_block = lax.all_to_all(filtered, "band", split_axis=0, concat_axis=1, tiled=True)
    local_gram = jnp.dot(
        row_block.T, row_block, precision=lax.Precision.HIGHEST, preferred_element_type=jnp.float32
    )
    gram = lax.psum(local_gram, ("space", "band"))
    scale = jnp.trace(gram) / VECTORS
    normed = gram / scale
    single = jnp.dot(
        row_block, normed, precision=lax.Precision.HIGHEST, preferred_element_type=jnp.float32
    )
    double = jnp.dot(
        single, normed, precision=lax.Precision.HIGHEST, preferred_element_type=jnp.float32
    )
    turned = (15.0 * row_block - 10.0 * single + 3.0 * double) / 8.0
    turned = turned * jnp.sqrt(order / scale)
    return lax.all_to_all(turned, "band", split_axis=1, concat_axis=0, tiled=True)


def solution(mesh):
    return jax.shard_map(
        per_device,
        mesh=mesh,
        in_specs=(P("space", "band"), P("space", None, None, None), P("space", None)),
        out_specs=P("space", "band"),
        check_vma=False,
    )
```

profile of v0, /device:TPU:0, one launch (start us, length us, event | category | flops | bytes accessed | tf_op | source)
XLA Modules:
  0.0 554.7 jit_solution(12402549872393374268)
XLA Ops:
  6.5 1.3 fusion.8
  7.8 0.5 collective-permute-start
  8.3 2.9 collective-permute-start.1
  11.3 0.7 compare_select_fusion
  12.0 0.1 copy.7
  12.1 0.1 reshape.33
  12.2 8.9 %collective-permute-done = f32[512,256]{1,0:T(8,128)S(1)} collective-permute-done((f32[512,256]{1,0:T(8,128)S(1)}, f32[512,256]{1,0:T(8,128)S(1)}, u32[]{:S(2)}, u32[]{:S(2)}) %collective-permute-start) | collective-permute-done | bytes 524320 | tf_op jit(solution)/shard_map/ppermute | solution.py:17
  21.0 1.5 collective-permute-done.1
  22.5 4.8 pad_maximum_fusion
  27.4 15.1 %gather_fusion = f32[112,256,256]{2,1,0:T(8,128)} fusion(f32[20,256,256]{2,1,0:T(8,128)} %bitcast.42, s32[1024]{0:T(1024)S(1)} %pad_clamp_fusion), kind=kCustom, calls=%fused_computation | custom fusion | bytes 58720704 | tf_op jit(solution)/shard_map/gather | solution.py:39
  42.5 34.2 %fusion.9 = f32[16,256,256,1]{1,2,3,0:T(8,128)S(1)} fusion(f32[16,7,256,256]{3,2,1,0:T(8,128)} %bitcast.44, f32[16,7,256,256]{3,2,1,0:T(8,128)} %param.4), kind=kOutput, calls=%fused_computation.26 | convolution fusion | flops 22548578304 | bytes 62914560 | tf_op jit(solution)/shard_map/lkij,lkjm->lim/dot_general | solution.py:40
  76.7 0.8 fusion.2
  77.5 1.2 copy-done.2
  78.8 0.1 fusion.7
  78.8 1.8 collective-permute-start.2
  80.6 1.3 collective-permute-start.3
  81.9 11.2 %collective-permute-done.2 = f32[512,256]{1,0:T(8,128)S(1)} collective-permute-done((f32[512,256]{1,0:T(8,128)S(1)}, f32[512,256]{1,0:T(8,128)S(1)}, u32[]{:S(2)}, u32[]{:S(2)}) %collective-permute-start.2) | collective-permute-done | bytes 524320 | tf_op jit(solution)/shard_map/ppermute | solution.py:17
  93.1 2.6 pad_maximum_fusion.1
  95.8 15.1 %gather_fusion.1 = f32[112,256,256]{2,1,0:T(8,128)} fusion(f32[20,256,256]{2,1,0:T(8,128)} %bitcast.41, s32[1024]{0:T(1024)S(1)} %pad_clamp_fusion), kind=kCustom, calls=%fused_computation.1 | custom fusion | bytes 58720704 | tf_op jit(solution)/shard_map/gather | solution.py:39
  110.9 35.1 %fusion.10 = f32[16,256,256,1]{1,2,3,0:T(8,128)} fusion(f32[16,7,256,256]{3,2,1,0:T(8,128)} %bitcast.43, f32[16,7,256,256]{3,2,1,0:T(8,128)} %param.4), kind=kOutput, calls=%fused_computation.27 | convolution fusion | flops 22548578304 | bytes 62914560 | tf_op jit(solution)/shard_map/lkij,lkjm->lim/dot_general | solution.py:40
  146.0 5.0 fusion.1
  150.9 5.3 copy.8
  156.3 98.5 %all_to_all.38 = f32[4,1024,256]{1,2,0:T(8,128)S(1)} all-to-all(f32[4,1024,256]{1,2,0:T(8,128)} %copy.8), channel_id=1, replica_groups=mesh['space'=8,'band'=4] {'band'}, dimensions={0} | all-to-all | bytes 8388608 | tf_op jit(solution)/shard_map/all_to_all | solution.py:45
  254.7 2.0 copy-done.4
  256.7 14.8 %fusion.11 = f32[1024,1024]{1,0:T(8,128)} fusion(f32[1024,1024]{0,1:T(8,128)S(1)} %bitcast.47), kind=kOutput, calls=%fused_computation.28 | convolution fusion | flops 12884901888 | bytes 8388608 | tf_op jit(solution)/shard_map/dot_general | solution.py:46
  271.5 0.0 all-reduce.2.cloned.1.call-update
  271.5 140.5 %all-reduce.2.cloned.1.call-done = f32[1024,1024]{1,0:T(8,128)} async-done(((f32[1024,1024]{1,0:T(8,128)}), f32[1024,1024]{1,0:T(8,128)}) %all-reduce.2.cloned.1.call-update) | async-done | bytes 4194320 | tf_op jit(solution)/shard_map/psum | solution.py:49
  412.0 2.9 select_reduce_fusion
  415.6 17.2 %fusion.3 = f32[1024,1024]{0,1:T(8,128)S(1)} fusion(f32[1024,1024]{0,1:T(8,128)} %bitcast.48, f32[1024,1024]{1,0:T(8,128)} %all-reduce.2.cloned.1.call-done, f32[]{:T(128)S(6)} %div.25), kind=kOutput, calls=%fused_computation.13 | convolution fusion | flops 12885950464 | bytes 12582916 | tf_op jit(solution)/shard_map/dot_general | solution.py:52
  432.9 14.3 %add_multiply_fusion = f32[1024,1024]{0,1:T(8,128)S(1)} fusion(f32[1024,1024]{0,1:T(8,128)S(1)} %fusion.3, f32[1024,1024]{0,1:T(8,128)S(1)} %bitcast.49, f32[]{:T(128)S(6)} %mul.49, f32[1024,1024]{1,0:T(8,128)S(1)} %copy-done.6, f32[]{:T(128)S(6)} %div.25), kind=kOutput, calls=%fused_computation.8 | convolution fusion | flops 12892241920 | bytes 16777224 | tf_op jit(solution)/shard_map/dot_general | solution.py:55
  447.1 95.1 %all_to_all.39 = f32[1024,4,256]{0,2,1:T(8,128)} all-to-all(f32[1024,4,256]{0,2,1:T(8,128)S(1)} %bitcast.50), channel_id=1, replica_groups=mesh['space'=8,'band'=4] {'band'}, dimensions={1} | all-to-all | bytes 8388608 | tf_op jit(solution)/shard_map/all_to_all | solution.py:60
  542.2 5.4 copy.9
  (16 shorter events, 0.0 us)
Async XLA Ops:
  6.5 405.5 %all-reduce.2.cloned.1.call-start = ((), (), s32[]{:S(2)}) async-start(), calls=%async_computation.2 | async-start | bytes 8388608 | tf_op jit(solution)/shard_map/psum | solution.py:49
  7.8 13.2 %collective-permute-start = (f32[512,256]{1,0:T(8,128)S(1)}, f32[512,256]{1,0:T(8,128)S(1)}, u32[]{:S(2)}, u32[]{:S(2)}) collective-permute-start(f32[512,256]{1,0:T(8,128)S(1)} %get-tuple-element.7), channel_id=1, source_target_pairs={{0,4},{4,8},{8,12},{12,16},{16,20},{20,24},{24,28},{28,0},{1,5},{5... | collective-permute-start | bytes 1572872 | tf_op jit(solution)/shard_map/ppermute | solution.py:17
  8.3 14.2 %collective-permute-start.1 = (f32[512,256]{1,0:T(8,128)S(1)}, f32[512,256]{1,0:T(8,128)S(1)}, u32[]{:S(2)}, u32[]{:S(2)}) collective-permute-start(f32[512,256]{1,0:T(8,128)S(1)} %get-tuple-element.8), channel_id=1, source_target_pairs={{4,0},{8,4},{12,8},{16,12},{20,16},{24,20},{28,24},{0,28},{5,1},{9... | collective-permute-start | bytes 1572872 | tf_op jit(solution)/shard_map/ppermute | solution.py:18
  42.5 34.2 %copy-start = (f32[4096,256]{1,0:T(8,128)S(1)}, f32[4096,256]{1,0:T(8,128)}, u32[]{:S(2)}) copy-start(f32[4096,256]{1,0:T(8,128)} %param.3) | copy-start | bytes 12582916
  76.7 2.1 copy-start.2
  78.8 14.3 %collective-permute-start.2 = (f32[512,256]{1,0:T(8,128)S(1)}, f32[512,256]{1,0:T(8,128)S(1)}, u32[]{:S(2)}, u32[]{:S(2)}) collective-permute-start(f32[512,256]{1,0:T(8,128)S(1)} %get-tuple-element.5), channel_id=1, source_target_pairs={{0,4},{4,8},{8,12},{12,16},{16,20},{20,24},{24,28},{28,0},{1,5},{5... | collective-permute-start | bytes 1572872 | tf_op jit(solution)/shard_map/ppermute | solution.py:17
  80.6 12.5 %collective-permute-start.3 = (f32[512,256]{1,0:T(8,128)S(1)}, f32[512,256]{1,0:T(8,128)S(1)}, u32[]{:S(2)}, u32[]{:S(2)}) collective-permute-start(f32[512,256]{1,0:T(8,128)S(1)} %get-tuple-element.6), channel_id=1, source_target_pairs={{4,0},{8,4},{12,8},{16,12},{20,16},{24,20},{28,24},{0,28},{5,1},{9... | collective-permute-start | bytes 1572872 | tf_op jit(solution)/shard_map/ppermute | solution.py:18
  110.9 35.1 %copy-start.1 = (f32[4096,256]{1,0:T(8,128)S(1)}, f32[4096,256]{1,0:T(8,128)}, u32[]{:S(2)}) copy-start(f32[4096,256]{1,0:T(8,128)} %param.3) | copy-start | bytes 12582916
  110.9 35.1 %copy-start.3 = (f32[16,256,256,1]{1,2,3,0:T(8,128)S(1)}, f32[16,256,256,1]{1,2,3,0:T(8,128)}, u32[]{:S(2)}) copy-start(f32[16,256,256,1]{1,2,3,0:T(8,128)} %copy-done.2) | copy-start | bytes 12582916
  254.7 2.0 copy-start.4
  415.6 17.3 %copy-start.5 = (f32[4,1024,256]{1,2,0:T(8,128)S(1)}, f32[4,1024,256]{1,2,0:T(8,128)}, u32[]{:S(2)}) copy-start(f32[4,1024,256]{1,2,0:T(8,128)} %copy-done.4) | copy-start | bytes 12582916
  415.6 17.3 %copy-start.6 = (f32[1024,1024]{1,0:T(8,128)S(1)}, f32[1024,1024]{1,0:T(8,128)}, u32[]{:S(2)}) copy-start(f32[1024,1024]{1,0:T(8,128)} %all-reduce.2.cloned.1.call-done) | copy-start | bytes 12582916
Sparse Core Ops, SparseCore 0:
  271.7 140.3 all-reduce.1
where the time goes:
time: 563 us; the launch traced here: 555 us
  blocking collectives  194 us (34%)
  waiting for transfers between devices  162 us (29%)
  matrix products  116 us (21%)
  local copies, waits for them, and re-layouts  45.7 us (8%)
  other arithmetic  16.9 us (3%)
  between operations  14.4 us (3%)
  starting transfers between devices  6.54 us (1%)
    psum x1, waiting for transfers between devices, per_device(): gram = lax.psum(local_gram, ('space', 'band'))  140 us
    all_to_all x1, blocking collectives, per_device(): lax.all_to_all(filtered, 'band', split_axis=0, concat_axis=1, tiled=True)  98.5 us
    all_to_all x1, blocking collectives, per_device(): lax.all_to_all(turned, 'band', split_axis=1, concat_axis=0, tiled=True)  95.1 us
    dot_general x2, matrix products, apply_operator(): jnp.einsum('lkij,lkjm->lim', blocks, picked, precision=lax.Precision.HIGH...  69.2 us
    gather x2, local copies, waits for them, and re-layouts, apply_operator(): picked = padded[slots]  30.2 us
    ppermute x2, waiting for transfers between devices, padded_2(): before = lax.ppermute(last, axis, up)  20.1 us
    dot_general x1, matrix products, per_device(): jnp.dot(row_block, normed, precision=lax.Precision.HIGHEST, preferred_ele...  17.2 us
    dot_general x1, matrix products, per_device(): jnp.dot(row_block.T, row_block, precision=lax.Precision.HIGHEST, preferre...  14.8 us
  transfers between devices with their start and end apart: 5, of which 4 were waited for; matrix products, arithmetic and copies ran while one was open for 0% of the time, Pallas kernels for 0%

commit v1 on v0

v1 whole, which is shorter than its diff:
```python
import functools

import jax
import jax.numpy as jnp
from jax import lax
from jax.experimental import pallas as pl
from jax.experimental.pallas import tpu as pltpu
from jax.sharding import PartitionSpec as P

REACH = 2
SPAN = 2 * REACH + 1
LANES = 128
MESH = pl.DeviceIdType.MESH
F32 = jnp.float32
BF16 = jnp.bfloat16


def split(x):
    high = x.astype(BF16)
    return high, (x - high.astype(F32)).astype(BF16)


def dot3(a, b):
    (ah, al), (bh, bl) = a, b
    mul = functools.partial(jnp.dot, preferred_element_type=F32)
    return mul(ah, bh) + (mul(ah, bl) + mul(al, bh))


def combine_kernel(slots, blocks, high, low, total):
    e = pl.program_id(0)
    basis = blocks.shape[2]
    total[0] = blocks[0, 1]
    total[SPAN - 1] = blocks[0, 2]
    for o in range(1, SPAN - 1):
        total[o] = jnp.zeros((basis, basis), F32)
    for k in range(blocks.shape[1]):
        if k not in (1, 2):
            slot = slots[e, k]
            total[slot] += blocks[0, k]
    for o in range(SPAN):
        high[0, :, o * basis:(o + 1) * basis], low[0, :, o * basis:(o + 1) * basis] = split(total[o])


def combine(slots, blocks):
    elem, count, basis, _ = blocks.shape
    out = jax.ShapeDtypeStruct((elem, basis, SPAN * basis), BF16)
    spec = pl.BlockSpec((1, basis, SPAN * basis), lambda e, s: (e, 0, 0))
    return pl.pallas_call(
        combine_kernel,
        grid_spec=pltpu.PrefetchScalarGridSpec(
            num_scalar_prefetch=1,
            grid=(elem,),
            in_specs=[pl.BlockSpec((1, count, basis, basis), lambda e, s: (e, 0, 0, 0))],
            out_specs=[spec, spec],
            scratch_shapes=[pltpu.VMEM((SPAN, basis, basis), F32)],
        ),
        out_shape=[out, out],
        compiler_params=pltpu.CompilerParams(vmem_limit_bytes=32 * 2**20),
        name="combine",
    )(slots, blocks)


def main_kernel(
    n_s, n_b, elem, basis, panel, parts,
    v_hbm, wh_hbm, wl_hbm, out,
    x, xh, xl, fh, fl, wh, wl, f1, recv, g, ar, whole, halo,
    load_sem, w_sem, halo_send, halo_recv, a2a_send, a2a_recv, ar_send, ar_recv,
    back_send, back_recv, own_sem,
):
    s, b = lax.axis_index("space"), lax.axis_index("band")
    per_home = elem // n_b
    home_rows = per_home * basis
    edge = REACH * basis
    vectors = n_b * panel
    order = n_s * elem * basis
    up, down = lax.rem(s + 1, n_s), lax.rem(s + n_s - 1, n_s)

    def rows_of(e):
        return pl.ds(pl.multiple_of(e * basis, basis), basis)

    def band_at(d):
        return lax.rem(b + d, n_b)

    def xor(index, bit):
        return index + bit * (1 - 2 * lax.rem(index // bit, 2))

    space_bits = [1 << k for k in range(n_s.bit_length() - 1)]
    band_bits = [1 << k for k in range(n_b.bit_length() - 1)]

    loads = [pltpu.make_async_copy(v_hbm, x, load_sem)]
    loads[0].start()

    def w_copies(e):
        return (
            pltpu.make_async_copy(wh_hbm.at[e], wh.at[e], w_sem.at[0, e]),
            pltpu.make_async_copy(wl_hbm.at[e], wl.at[e], w_sem.at[1, e]),
        )

    def start_w(e, carry):
        for copy in w_copies(e):
            copy.start()
        return carry

    lax.fori_loop(0, elem, start_w, 0)

    barrier = pltpu.get_barrier_semaphore()
    peers = [(up, b), (down, b)]
    peers += [(s, band_at(d)) for d in range(1, n_b)]
    peers += [(xor(s, bit), b) for bit in space_bits]
    for peer in peers:
        pl.semaphore_signal(barrier, inc=1, device_id=peer, device_id_type=MESH)
    pl.semaphore_wait(barrier, len(peers))

    def halo_copies(step, field):
        def copy(src, side, target):
            return pltpu.make_async_remote_copy(
                src_ref=src, dst_ref=halo.at[step, side],
                send_sem=halo_send.at[step, side], recv_sem=halo_recv.at[step, side],
                device_id=(target, b), device_id_type=MESH)
        last = field.at[pl.ds(elem * basis - edge, edge)]
        first = field.at[pl.ds(0, edge)]
        return copy(last, 0, up), copy(first, 1, down)

    def take_halo(step, copies, high, low):
        for side, copy in enumerate(copies):
            copy.wait_recv()
            start = side * (elem + REACH) * basis
            high[pl.ds(start, edge)], low[pl.ds(start, edge)] = split(halo[step, side])

    def applied(e, high, low):
        near = pl.ds(pl.multiple_of(e * basis, basis), SPAN * basis)
        return dot3((wh[e], wl[e]), (high[near], low[near]))

    loads[0].wait()
    halo1 = halo_copies(0, x)
    for copy in halo1:
        copy.start()

    def split_x(e, carry):
        at = rows_of(e + REACH)
        xh[at], xl[at] = split(x[rows_of(e)])
        return carry

    lax.fori_loop(0, elem, split_x, 0)

    def first_apply(e, carry):
        for copy in w_copies(e):
            copy.wait()
        value = (applied(e, xh, xl) - 0.5 * x[rows_of(e)]) / 1.5
        f1[rows_of(e)] = value
        at = rows_of(e + REACH)
        fh[at], fl[at] = split(value)
        return carry

    ahead = REACH + (elem - 2 * REACH) // 3
    lax.fori_loop(REACH, ahead, first_apply, 0)
    take_halo(0, halo1, xh, xl)
    lax.fori_loop(0, REACH, first_apply, 0)
    lax.fori_loop(elem - REACH, elem, first_apply, 0)
    halo2 = halo_copies(1, f1)
    for copy in halo2:
        copy.start()
    lax.fori_loop(ahead, elem - REACH, first_apply, 0)
    for copy in halo1:
        copy.wait_send()
    take_halo(1, halo2, fh, fl)

    def filtered_of(e):
        mine = rows_of(e)
        return 2.0 * (applied(e, fh, fl) - 0.5 * f1[mine]) / 1.5 - x[mine]

    def to_home(c, d):
        home = band_at(d)
        return pltpu.make_async_remote_copy(
            src_ref=x.at[rows_of(home * per_home + c)],
            dst_ref=recv.at[rows_of(b * per_home + c)],
            send_sem=a2a_send.at[c, d], recv_sem=a2a_recv.at[c, b],
            device_id=(s, home), device_id_type=MESH)

    far_first = sorted(range(1, n_b), key=lambda d: -min(d, n_b - d))

    def second_apply(c, carry):
        for d in far_first:
            e = band_at(d) * per_home + c
            x[rows_of(e)] = filtered_of(e)
            to_home(c, d).start()
        e = b * per_home + c
        recv[rows_of(e)] = filtered_of(e)
        return carry

    lax.fori_loop(0, per_home, second_apply, 0)
    for copy in halo2:
        copy.wait_send()

    pairs = [(i, j) for i in range(n_b) for j in range(i, n_b)]
    cuts = panel // LANES
    g[...] = jnp.zeros_like(g)

    def from_home(c, d):
        source = band_at(d)
        return pltpu.make_async_remote_copy(
            src_ref=x.at[rows_of(c)],
            dst_ref=recv.at[rows_of(source * per_home + c)],
            send_sem=a2a_send.at[c, d], recv_sem=a2a_recv.at[c, source],
            device_id=(s, source), device_id_type=MESH)

    def add_gram(c, carry):
        for d in range(1, n_b):
            from_home(c, d).wait_recv()
        parts_of = []
        for i in range(n_b):
            at = rows_of(i * per_home + c)
            high, low = split(recv[at])
            xh[at], xl[at] = high, low
            parts_of.append((high, low))
        for i in range(n_b):
            turned = split(recv[rows_of(i * per_home + c)].T)
            for j in range(i, n_b):
                product = dot3(turned, parts_of[j])
                t = pairs.index((i, j))
                for cut in range(cuts):
                    g[pl.ds((t * cuts + cut) * panel, panel)] += product[:, cut * LANES:(cut + 1) * LANES]
        return carry

    lax.fori_loop(0, per_home, add_gram, 0)

    length = g.shape[0] // parts
    orders = []
    for part in range(parts):
        low_bits, high_bits = [("s", bit) for bit in space_bits], [("b", bit) for bit in band_bits]
        if part % 2:
            low_bits, high_bits = low_bits[:1] + low_bits[1:][::-1], high_bits[::-1]
        orders.append(low_bits + high_bits)
    steps = len(orders[0])

    def partner(kind, bit):
        if kind == "s":
            return (xor(s, bit), b), lax.rem(s // bit, 2)
        return (s, xor(b, bit)), lax.rem(b // bit, 2)

    starts = [part * length for part in range(parts)]
    trail = []
    offset = 0
    for k in range(steps):
        half = length >> (k + 1)
        copies, keeps = [], []
        for part in range(parts):
            target, bit = partner(*orders[part][k])
            keep = pl.multiple_of(starts[part] + bit * half, 8)
            give = pl.multiple_of(starts[part] + (1 - bit) * half, 8)
            copy = pltpu.make_async_remote_copy(
                src_ref=g.at[pl.ds(give, half)], dst_ref=ar.at[part, pl.ds(offset, half)],
                send_sem=ar_send.at[0, k, part], recv_sem=ar_recv.at[0, k, part],
                device_id=target, device_id_type=MESH)
            copy.start()
            copies.append(copy)
            keeps.append((keep, give))
        for part in range(parts):
            copies[part].wait()
            g[pl.ds(keeps[part][0], half)] += ar[part, pl.ds(offset, half)]
            starts[part] = keeps[part][0]
        trail.append(keeps)
        offset += half
    for part in range(parts):
        own = pl.ds(starts[part], length >> steps)
        whole[own] = g[own]
    for k in reversed(range(steps)):
        half = length >> (k + 1)
        copies = []
        for part in range(parts):
            target, _ = partner(*orders[part][k])
            keep, give = trail[k][part]
            copy = pltpu.make_async_remote_copy(
                src_ref=whole.at[pl.ds(keep, half)], dst_ref=whole.at[pl.ds(keep, half)],
                send_sem=ar_send.at[1, k, part], recv_sem=ar_recv.at[1, k, part],
                device_id=target, device_id_type=MESH)
            copy.start()
            copies.append(copy)
        for copy in copies:
            copy.wait()

    def gram_block(t):
        return jnp.concatenate(
            [whole[pl.ds((t * cuts + cut) * panel, panel)] for cut in range(cuts)], axis=1)

    eye = (lax.broadcasted_iota(jnp.int32, (panel, panel), 0)
           == lax.broadcasted_iota(jnp.int32, (panel, panel), 1))
    trace = sum(
        jnp.sum(jnp.where(eye, gram_block(pairs.index((i, i))), 0.0), keepdims=True)
        for i in range(n_b))
    scale = trace / vectors
    slabs = vectors // basis

    def put(first, row, column, value):
        slab, at = row // basis, row % basis
        high, low = split(value)
        wh[first + slab, at:at + panel, column:column + panel] = high
        wl[first + slab, at:at + panel, column:column + panel] = low

    for t, (i, j) in enumerate(pairs):
        normed = gram_block(t) / scale
        put(0, i * panel, j * panel, normed)
        if i != j:
            put(0, j * panel, i * panel, normed.T)

    def matrix(first):
        return tuple(
            ref[first:first + slabs, :, :vectors].reshape(vectors, vectors) for ref in (wh, wl))

    def polynomial(r, carry):
        high, low = wh[r, :, :vectors], wl[r, :, :vectors]
        squared = dot3((high, low), matrix(0))
        normed = high.astype(F32) + low.astype(F32)
        shape = (basis, vectors)
        row = lax.broadcasted_iota(jnp.int32, shape, 0) + r * basis
        diagonal = jnp.where(row == lax.broadcasted_iota(jnp.int32, shape, 1), 15.0, 0.0)
        value = split((diagonal - 10.0 * normed + 3.0 * squared) / 8.0)
        wh[slabs + r, :, :vectors], wl[slabs + r, :, :vectors] = value
        return carry

    lax.fori_loop(0, slabs, polynomial, 0)
    gain = jnp.sqrt(order / scale)

    def back(c, d):
        owner = band_at(d)
        return pltpu.make_async_remote_copy(
            src_ref=f1.at[rows_of(owner * per_home + c)],
            dst_ref=out.at[rows_of(b * per_home + c)],
            send_sem=back_send.at[c, d], recv_sem=back_recv.at[c, b],
            device_id=(s, owner), device_id_type=MESH)

    def own_back(c):
        at = rows_of(b * per_home + c)
        return pltpu.make_async_copy(f1.at[at], out.at[at], own_sem.at[c])

    def rotate(c, carry):
        left = tuple(
            jnp.concatenate([ref[rows_of(i * per_home + c)] for i in range(n_b)], axis=1)
            for ref in (xh, xl))
        turned = dot3(left, matrix(slabs)) * gain
        for i in range(n_b):
            f1[rows_of(i * per_home + c)] = turned[:, i * panel:(i + 1) * panel]
        for d in far_first:
            back(c, d).start()
        own_back(c).start()
        return carry

    lax.fori_loop(0, per_home, rotate, 0)

    def finish(c, carry):
        for d in range(1, n_b):
            to_home(c, d).wait_send()
            back(c, d).wait_send()
            source = band_at(d)
            pltpu.make_async_remote_copy(
                src_ref=f1.at[rows_of(c)],
                dst_ref=out.at[rows_of(source * per_home + c)],
                send_sem=back_send.at[c, d], recv_sem=back_recv.at[c, source],
                device_id=(s, source), device_id_type=MESH).wait_recv()
        own_back(c).wait()
        return carry

    lax.fori_loop(0, per_home, finish, 0)


def per_device(n_s, n_b, vectors, blocks, neighbours):
    elem, _, basis, _ = blocks.shape
    panel = vectors.shape[1]
    total = elem * n_s
    ids = lax.axis_index("space") * elem + jnp.arange(elem, dtype=jnp.int32)
    slots = (neighbours - ids[:, None] + REACH + total) % total
    high, low = combine(slots, blocks)

    rows = elem * basis
    per_home = elem // n_b
    devices = n_s * n_b
    need = n_b * (n_b + 1) // 2 * (panel // LANES) * panel
    parts = 2 if need % (16 * devices) == 0 else 1
    unit = 8 * devices * parts
    packed = -(-need // unit) * unit
    steps = devices.bit_length() - 1
    padded = (elem + 2 * REACH) * basis
    dma = pltpu.SemaphoreType.DMA
    any_spec = pl.BlockSpec(memory_space=pl.ANY)
    flops = 2 * rows * panel * 3 * (2 * SPAN * basis) + 6 * rows * panel * 1024 * 3
    return pl.pallas_call(
        functools.partial(main_kernel, n_s, n_b, elem, basis, panel, parts),
        out_shape=jax.ShapeDtypeStruct((rows, panel), F32),
        in_specs=[any_spec] * 3,
        out_specs=any_spec,
        scratch_shapes=[
            pltpu.VMEM((rows, panel), F32),
            pltpu.VMEM((padded, panel), BF16),
            pltpu.VMEM((padded, panel), BF16),
            pltpu.VMEM((padded, panel), BF16),
            pltpu.VMEM((padded, panel), BF16),
            pltpu.VMEM((elem, basis, SPAN * basis), BF16),
            pltpu.VMEM((elem, basis, SPAN * basis), BF16),
            pltpu.VMEM((rows, panel), F32),
            pltpu.VMEM((rows, panel), F32),
            pltpu.VMEM((packed, LANES), F32),
            pltpu.VMEM((parts, packed // parts, LANES), F32),
            pltpu.VMEM((packed, LANES), F32),
            pltpu.VMEM((2, 2, REACH * basis, panel), F32),
            dma, dma((2, elem)), dma((2, 2)), dma((2, 2)),
            dma((per_home, n_b)), dma((per_home, n_b)),
            dma((2, steps, parts)), dma((2, steps, parts)),
            dma((per_home, n_b)), dma((per_home, n_b)), dma((per_home,)),
        ],
        compiler_params=pltpu.CompilerParams(
            collective_id=0, has_side_effects=True, vmem_limit_bytes=60 * 2**20),
        cost_estimate=pl.CostEstimate(
            flops=flops, bytes_accessed=40 * 2**20, transcendentals=0),
        name="filter_and_rotate",
    )(vectors, high, low)


def solution(mesh):
    return jax.shard_map(
        functools.partial(per_device, mesh.shape["space"], mesh.shape["band"]),
        mesh=mesh,
        in_specs=(P("space", "band"), P("space", None, None, None), P("space", None)),
        out_specs=P("space", "band"),
        check_vma=False,
    )
```

time: 563 us -> 312 us (0.55)
  the two profiles are of different devices: /device:TPU:0 before, /device:TPU:9 now
where the time goes in v1:
time: 312 us; the launch traced here: 311 us
  Pallas kernels  298 us (96%)
  local copies, waits for them, and re-layouts  13 us (4%)
    pallas_call x1, Pallas kernels, per_device(): pl.pallas_call(functools.partial(main_kernel, n_s, n_b, elem, basis, pane...  280 us
    pallas_call x1, Pallas kernels, combine(): pl.pallas_call(combine_kernel, grid_spec=pltpu.PrefetchScalarGridSpec(num...  18.2 us
    unnamed x6, local copies, waits for them, and re-layouts  13 us

profile of v1, /device:TPU:9, one launch (start us, length us, event | category | flops | bytes accessed | tf_op | source)
XLA Modules:
  0.0 311.4 jit_solution(8685275814944424556)
XLA Ops:
  0.0 0.8 copy.4
  0.8 0.1 add_select_fusion.slots
  0.8 18.2 %combine.1 = (bf16[16,256,1280]{2,1,0:T(8,128)(2,1)S(1)}, bf16[16,256,1280]{2,1,0:T(8,128)(2,1)S(1)}) custom-call(s32[16,7]{1,0:T(8,128)S(1)} %add_select_fusion.slots, f32[16,7,256,256]{3,2,1,0:T(8,128)} %blocks.1), custom_call_target="tpu_custom_call" | custom-call | tf_op jit(solution)/shard_map/combine/pallas_call | solution.py:48
  19.0 0.0 copy-start
  19.0 4.0 %copy-done = bf16[16,256,1280]{2,1,0:T(8,128)(2,1)} copy-done((bf16[16,256,1280]{2,1,0:T(8,128)(2,1)}, bf16[16,256,1280]{2,1,0:T(8,128)(2,1)S(1)}, u32[]{:S(2)}) %copy-start) | copy-done | bytes 10485784
  23.0 0.0 copy-start.1
  23.0 3.8 %copy-done.1 = bf16[16,256,1280]{2,1,0:T(8,128)(2,1)} copy-done((bf16[16,256,1280]{2,1,0:T(8,128)(2,1)}, bf16[16,256,1280]{2,1,0:T(8,128)(2,1)S(1)}, u32[]{:S(2)}) %copy-start.1) | copy-done | bytes 10485784
  26.8 280.1 %filter_and_rotate.1 = f32[4096,256]{1,0:T(8,128)} custom-call(f32[4096,256]{1,0:T(8,128)} %v_hbm.1, bf16[16,256,1280]{2,1,0:T(8,128)(2,1)} %copy-done, bf16[16,256,1280]{2,1,0:T(8,128)(2,1)} %copy-done.1), custom_call_target="tpu_custom_call" | custom-call | flops 35433480192 | bytes 41943040 | tf_op jit(solution)/shard_map/filter_and_rotate/pallas_call | solution.py:386
  306.9 4.5 %copy.6 = f32[4096,256]{1,0:T(8,128)} copy(f32[4096,256]{1,0:T(8,128)} %filter_and_rotate.1) | data formatting | bytes 8388608
  (1 shorter events, 0.0 us)
Async XLA Ops:
  19.0 4.0 %copy-start = (bf16[16,256,1280]{2,1,0:T(8,128)(2,1)}, bf16[16,256,1280]{2,1,0:T(8,128)(2,1)S(1)}, u32[]{:S(2)}) copy-start(bf16[16,256,1280]{2,1,0:T(8,128)(2,1)S(1)} %get-tuple-element.7.wh_hbm) | copy-start | bytes 31457284
  23.0 3.8 %copy-start.1 = (bf16[16,256,1280]{2,1,0:T(8,128)(2,1)}, bf16[16,256,1280]{2,1,0:T(8,128)(2,1)S(1)}, u32[]{:S(2)}) copy-start(bf16[16,256,1280]{2,1,0:T(8,128)(2,1)S(1)} %get-tuple-element.8.wl_hbm) | copy-start | bytes 31457284

commit v2 on v1

--- a/solution.py
+++ b/solution.py
@@ -26,45 +26,12 @@
     return mul(ah, bh) + (mul(ah, bl) + mul(al, bh))
 
 
-def combine_kernel(slots, blocks, high, low, total):
-    e = pl.program_id(0)
-    basis = blocks.shape[2]
-    total[0] = blocks[0, 1]
-    total[SPAN - 1] = blocks[0, 2]
-    for o in range(1, SPAN - 1):
-        total[o] = jnp.zeros((basis, basis), F32)
-    for k in range(blocks.shape[1]):
-        if k not in (1, 2):
-            slot = slots[e, k]
-            total[slot] += blocks[0, k]
-    for o in range(SPAN):
-        high[0, :, o * basis:(o + 1) * basis], low[0, :, o * basis:(o + 1) * basis] = split(total[o])
-
-
-def combine(slots, blocks):
-    elem, count, basis, _ = blocks.shape
-    out = jax.ShapeDtypeStruct((elem, basis, SPAN * basis), BF16)
-    spec = pl.BlockSpec((1, basis, SPAN * basis), lambda e, s: (e, 0, 0))
-    return pl.pallas_call(
-        combine_kernel,
-        grid_spec=pltpu.PrefetchScalarGridSpec(
-            num_scalar_prefetch=1,
-            grid=(elem,),
-            in_specs=[pl.BlockSpec((1, count, basis, basis), lambda e, s: (e, 0, 0, 0))],
-            out_specs=[spec, spec],
-            scratch_shapes=[pltpu.VMEM((SPAN, basis, basis), F32)],
-        ),
-        out_shape=[out, out],
-        compiler_params=pltpu.CompilerParams(vmem_limit_bytes=32 * 2**20),
-        name="combine",
-    )(slots, blocks)
-
-
 def main_kernel(
     n_s, n_b, elem, basis, panel, parts,
-    v_hbm, wh_hbm, wl_hbm, out,
-    x, xh, xl, fh, fl, wh, wl, f1, recv, g, ar, whole, halo,
-    load_sem, w_sem, halo_send, halo_recv, a2a_send, a2a_recv, ar_send, ar_recv,
+    weights, v_hbm, blocks, out,
+    x, xh, xl, fh, fl, wh, wl, f1, recv, g, ar, whole, halo, raw,
+    load_sem, raw_sem, halo_send, halo_recv, a2a_send, a2a_recv, ar_send, ar_recv,
+    z_send, z_recv,
     back_send, back_recv, own_sem,
 ):
     s, b = lax.axis_index("space"), lax.axis_index("band")
@@ -85,23 +52,20 @@
         return index + bit * (1 - 2 * lax.rem(index // bit, 2))
 
     space_bits = [1 << k for k in range(n_s.bit_length() - 1)]
-    band_bits = [1 << k for k in range(n_b.bit_length() - 1)]
-
     loads = [pltpu.make_async_copy(v_hbm, x, load_sem)]
     loads[0].start()
 
-    def w_copies(e):
-        return (
-            pltpu.make_async_copy(wh_hbm.at[e], wh.at[e], w_sem.at[0, e]),
-            pltpu.make_async_copy(wl_hbm.at[e], wl.at[e], w_sem.at[1, e]),
-        )
-
-    def start_w(e, carry):
-        for copy in w_copies(e):
-            copy.start()
-        return carry
-
-    lax.fori_loop(0, elem, start_w, 0)
+    count, slots = blocks.shape[1], raw.shape[0]
+
+    def element_at(p):
+        return lax.rem(p + elem // 2, elem)
+
+    def raw_copy(p):
+        slot = lax.rem(p, slots)
+        return pltpu.make_async_copy(blocks.at[element_at(p)], raw.at[slot], raw_sem.at[slot])
+
+    for p in range(slots - 1):
+        raw_copy(jnp.int32(p)).start()
 
     barrier = pltpu.get_barrier_semaphore()
     peers = [(up, b), (down, b)]
@@ -143,24 +107,50 @@
 
     lax.fori_loop(0, elem, split_x, 0)
 
-    def first_apply(e, carry):
-        for copy in w_copies(e):
-            copy.wait()
+    tile = 32
+
+    def merge(p, e):
+        raw_copy(p).wait()
+
+        @pl.when(p + slots - 1 < elem)
+        def _():
+            raw_copy(p + slots - 1).start()
+
+        slot = lax.rem(p, slots)
+        weight = [
+            [weights[(e * count + k) * SPAN + o] for o in range(SPAN)] for k in range(count)]
+
+        def merge_rows(r, carry):
+            at = pl.ds(pl.multiple_of(r * tile, tile), tile)
+            blocks_at = [raw[slot, k, at, :] for k in range(count)]
+            for o in range(SPAN):
+                total = {0: blocks_at[1], SPAN - 1: blocks_at[2]}.get(o)
+                for k in range(count):
+                    if k not in (1, 2):
+                        term = blocks_at[k] * weight[k][o]
+                        total = term if total is None else total + term
+                columns = slice(o * basis, (o + 1) * basis)
+                wh[e, at, columns], wl[e, at, columns] = split(total)
+            return carry
+
+        lax.fori_loop(0, basis // tile, merge_rows, 0)
+
+    def first_apply(p, carry):
+        e = element_at(p)
+        merge(p, e)
         value = (applied(e, xh, xl) - 0.5 * x[rows_of(e)]) / 1.5
         f1[rows_of(e)] = value
         at = rows_of(e + REACH)
         fh[at], fl[at] = split(value)
         return carry
 
-    ahead = REACH + (elem - 2 * REACH) // 3
-    lax.fori_loop(REACH, ahead, first_apply, 0)
+    lax.fori_loop(0, elem // 2 - REACH, first_apply, 0)
     take_halo(0, halo1, xh, xl)
-    lax.fori_loop(0, REACH, first_apply, 0)
-    lax.fori_loop(elem - REACH, elem, first_apply, 0)
+    lax.fori_loop(elem // 2 - REACH, elem // 2 + REACH, first_apply, 0)
     halo2 = halo_copies(1, f1)
     for copy in halo2:
         copy.start()
-    lax.fori_loop(ahead, elem - REACH, first_apply, 0)
+    lax.fori_loop(elem // 2 + REACH, elem, first_apply, 0)
     for copy in halo1:
         copy.wait_send()
     take_halo(1, halo2, fh, fl)
@@ -225,18 +215,13 @@
     lax.fori_loop(0, per_home, add_gram, 0)
 
     length = g.shape[0] // parts
-    orders = []
-    for part in range(parts):
-        low_bits, high_bits = [("s", bit) for bit in space_bits], [("b", bit) for bit in band_bits]
-        if part % 2:
-            low_bits, high_bits = low_bits[:1] + low_bits[1:][::-1], high_bits[::-1]
-        orders.append(low_bits + high_bits)
-    steps = len(orders[0])
-
-    def partner(kind, bit):
-        if kind == "s":
-            return (xor(s, bit), b), lax.rem(s // bit, 2)
-        return (s, xor(b, bit)), lax.rem(b // bit, 2)
+    orders = [
+        space_bits[:1] + (space_bits[1:][::-1] if part % 2 else space_bits[1:])
+        for part in range(parts)]
+    steps = len(space_bits)
+
+    def partner(bit):
+        return (xor(s, bit), b), lax.rem(s // bit, 2)
 
     starts = [part * length for part in range(parts)]
     trail = []
@@ -245,7 +230,7 @@
         half = length >> (k + 1)
         copies, keeps = [], []
         for part in range(parts):
-            target, bit = partner(*orders[part][k])
+            target, bit = partner(orders[part][k])
             keep = pl.multiple_of(starts[part] + bit * half, 8)
             give = pl.multiple_of(starts[part] + (1 - bit) * half, 8)
             copy = pltpu.make_async_remote_copy(
@@ -254,22 +239,53 @@
                 device_id=target, device_id_type=MESH)
             copy.start()
             copies.append(copy)
-            keeps.append((keep, give))
+            keeps.append(keep)
         for part in range(parts):
             copies[part].wait()
-            g[pl.ds(keeps[part][0], half)] += ar[part, pl.ds(offset, half)]
-            starts[part] = keeps[part][0]
+            g[pl.ds(keeps[part], half)] += ar[part, pl.ds(offset, half)]
+            starts[part] = keeps[part]
         trail.append(keeps)
         offset += half
+    piece = (length >> steps) // n_b
+
+    def piece_at(part, index):
+        return pl.ds(pl.multiple_of(starts[part] + index * piece, 8), piece)
+
+    copies = []
     for part in range(parts):
-        own = pl.ds(starts[part], length >> steps)
-        whole[own] = g[own]
+        for d in range(1, n_b):
+            target = band_at(d)
+            copy = pltpu.make_async_remote_copy(
+                src_ref=g.at[piece_at(part, target)],
+                dst_ref=ar.at[part, pl.ds(offset + (d - 1) * piece, piece)],
+                send_sem=z_send.at[0, d, part], recv_sem=z_recv.at[0, d, part],
+                device_id=(s, target), device_id_type=MESH)
+            copy.start()
+            copies.append(copy)
+    for copy in copies:
+        copy.wait()
+    copies = []
+    for part in range(parts):
+        own = piece_at(part, b)
+        total = g[own]
+        for d in range(1, n_b):
+            total = total + ar[part, pl.ds(offset + (d - 1) * piece, piece)]
+        whole[own] = total
+        for d in range(1, n_b):
+            copy = pltpu.make_async_remote_copy(
+                src_ref=whole.at[own], dst_ref=whole.at[own],
+                send_sem=z_send.at[1, d, part], recv_sem=z_recv.at[1, d, part],
+                device_id=(s, band_at(d)), device_id_type=MESH)
+            copy.start()
+            copies.append(copy)
+    for copy in copies:
+        copy.wait()
     for k in reversed(range(steps)):
         half = length >> (k + 1)
         copies = []
         for part in range(parts):
-            target, _ = partner(*orders[part][k])
-            keep, give = trail[k][part]
+            target, _ = partner(orders[part][k])
+            keep = trail[k][part]
             copy = pltpu.make_async_remote_copy(
                 src_ref=whole.at[pl.ds(keep, half)], dst_ref=whole.at[pl.ds(keep, half)],
                 send_sem=ar_send.at[1, k, part], recv_sem=ar_recv.at[1, k, part],
@@ -289,36 +305,26 @@
         jnp.sum(jnp.where(eye, gram_block(pairs.index((i, i))), 0.0), keepdims=True)
         for i in range(n_b))
     scale = trace / vectors
-    slabs = vectors // basis
-
-    def put(first, row, column, value):
-        slab, at = row // basis, row % basis
-        high, low = split(value)
-        wh[first + slab, at:at + panel, column:column + panel] = high
-        wl[first + slab, at:at + panel, column:column + panel] = low
+    def put(i, j, value):
+        columns = slice(j * panel, (j + 1) * panel)
+        wh[i, :panel, columns], wl[i, :panel, columns] = split(value)
 
     for t, (i, j) in enumerate(pairs):
         normed = gram_block(t) / scale
-        put(0, i * panel, j * panel, normed)
+        put(i, j, normed)
         if i != j:
-            put(0, j * panel, i * panel, normed.T)
-
-    def matrix(first):
-        return tuple(
-            ref[first:first + slabs, :, :vectors].reshape(vectors, vectors) for ref in (wh, wl))
-
-    def polynomial(r, carry):
-        high, low = wh[r, :, :vectors], wl[r, :, :vectors]
-        squared = dot3((high, low), matrix(0))
+            put(j, i, normed.T)
+
+    def polynomial(i):
+        high, low = wh[i, :panel, :vectors], wl[i, :panel, :vectors]
+        matrix = tuple(ref[:n_b, :panel, :vectors].reshape(vectors, vectors) for ref in (wh, wl))
+        squared = dot3((high, low), matrix)
         normed = high.astype(F32) + low.astype(F32)
-        shape = (basis, vectors)
-        row = lax.broadcasted_iota(jnp.int32, shape, 0) + r * basis
+        shape = (panel, vectors)
+        row = lax.broadcasted_iota(jnp.int32, shape, 0) + i * panel
         diagonal = jnp.where(row == lax.broadcasted_iota(jnp.int32, shape, 1), 15.0, 0.0)
-        value = split((diagonal - 10.0 * normed + 3.0 * squared) / 8.0)
-        wh[slabs + r, :, :vectors], wl[slabs + r, :, :vectors] = value
-        return carry
-
-    lax.fori_loop(0, slabs, polynomial, 0)
+        return split(((diagonal - 10.0 * normed + 3.0 * squared) / 8.0).T)
+
     gain = jnp.sqrt(order / scale)
 
     def back(c, d):
@@ -333,19 +339,23 @@
         at = rows_of(b * per_home + c)
         return pltpu.make_async_copy(f1.at[at], out.at[at], own_sem.at[c])
 
-    def rotate(c, carry):
-        left = tuple(
-            jnp.concatenate([ref[rows_of(i * per_home + c)] for i in range(n_b)], axis=1)
-            for ref in (xh, xl))
-        turned = dot3(left, matrix(slabs)) * gain
-        for i in range(n_b):
-            f1[rows_of(i * per_home + c)] = turned[:, i * panel:(i + 1) * panel]
-        for d in far_first:
-            back(c, d).start()
-        own_back(c).start()
-        return carry
-
-    lax.fori_loop(0, per_home, rotate, 0)
+    def rotate(d, send):
+        i = band_at(d)
+        poly = polynomial(i)
+
+        def rotate_rows(c, carry):
+            left = tuple(
+                jnp.concatenate([ref[rows_of(k * per_home + c)] for k in range(n_b)], axis=1)
+                for ref in (xh, xl))
+            f1[rows_of(i * per_home + c)] = dot3(left, poly) * gain
+            send(c, d).start()
+            return carry
+
+        lax.fori_loop(0, per_home, rotate_rows, 0)
+
+    for d in far_first:
+        rotate(d, back)
+    rotate(0, lambda c, d: own_back(c))
 
     def finish(c, carry):
         for d in range(1, n_b):
@@ -364,12 +374,12 @@
 
 
 def per_device(n_s, n_b, vectors, blocks, neighbours):
-    elem, _, basis, _ = blocks.shape
+    elem, count, basis, _ = blocks.shape
     panel = vectors.shape[1]
     total = elem * n_s
     ids = lax.axis_index("space") * elem + jnp.arange(elem, dtype=jnp.int32)
     slots = (neighbours - ids[:, None] + REACH + total) % total
-    high, low = combine(slots, blocks)
+    weights = jax.nn.one_hot(slots, SPAN, dtype=F32).reshape(-1)
 
     rows = elem * basis
     per_home = elem // n_b
@@ -378,7 +388,7 @@
     parts = 2 if need % (16 * devices) == 0 else 1
     unit = 8 * devices * parts
     packed = -(-need // unit) * unit
-    steps = devices.bit_length() - 1
+    steps = n_s.bit_length() - 1
     padded = (elem + 2 * REACH) * basis
     dma = pltpu.SemaphoreType.DMA
     any_spec = pl.BlockSpec(memory_space=pl.ANY)
@@ -386,7 +396,7 @@
     return pl.pallas_call(
         functools.partial(main_kernel, n_s, n_b, elem, basis, panel, parts),
         out_shape=jax.ShapeDtypeStruct((rows, panel), F32),
-        in_specs=[any_spec] * 3,
+        in_specs=[pl.BlockSpec(memory_space=pltpu.SMEM), any_spec, any_spec],
         out_specs=any_spec,
         scratch_shapes=[
             pltpu.VMEM((rows, panel), F32),
@@ -402,9 +412,11 @@
             pltpu.VMEM((parts, packed // parts, LANES), F32),
             pltpu.VMEM((packed, LANES), F32),
             pltpu.VMEM((2, 2, REACH * basis, panel), F32),
-            dma, dma((2, elem)), dma((2, 2)), dma((2, 2)),
+            pltpu.VMEM((3, count, basis, basis), F32),
+            dma, dma((3,)), dma((2, 2)), dma((2, 2)),
             dma((per_home, n_b)), dma((per_home, n_b)),
             dma((2, steps, parts)), dma((2, steps, parts)),
+            dma((2, n_b, parts)), dma((2, n_b, parts)),
             dma((per_home, n_b)), dma((per_home, n_b)), dma((per_home,)),
         ],
         compiler_params=pltpu.CompilerParams(
@@ -412,7 +424,7 @@
         cost_estimate=pl.CostEstimate(
             flops=flops, bytes_accessed=40 * 2**20, transcendentals=0),
         name="filter_and_rotate",
-    )(vectors, high, low)
+    )(weights, vectors, blocks)
 
 
 def solution(mesh):

time: 312 us -> 278 us (0.89)
  Pallas kernels: 298 us -> 271 us
  local copies, waits for them, and re-layouts: 13 us -> 5.33 us
    pallas_call x1 -> x0, Pallas kernels: 18.2 us -> none  [combine(): pl.pallas_call(combine_kernel, grid_spec=pltpu.PrefetchScalarGridSpec(num...]
    pallas_call x1, Pallas kernels: 280 us -> 271 us  [per_device(): pl.pallas_call(functools.partial(main_kernel, n_s, n_b, elem, basis, pane...]
    unnamed x6 -> x1, local copies, waits for them, and re-layouts: 13 us -> 4.47 us
where the time goes in v2:
time: 278 us; the launch traced here: 277 us
  Pallas kernels  271 us (97%)
  local copies, waits for them, and re-layouts  5.33 us (2%)
    pallas_call x1, Pallas kernels, per_device(): pl.pallas_call(functools.partial(main_kernel, n_s, n_b, elem, basis, pane...  271 us

profile of v2, /device:TPU:9, one launch (start us, length us, event | category | flops | bytes accessed | tf_op | source)
XLA Modules:
  0.0 277.1 jit_solution(13270064779560405063)
XLA Ops:
  0.0 0.7 add_select_fusion
  0.7 0.1 copy.5
  0.8 0.1 fusion
  0.9 0.8 reshape.11.weights
  1.7 271.0 %filter_and_rotate.1 = f32[4096,256]{1,0:T(8,128)} custom-call(f32[560]{0:T(1024)} %reshape.11.weights, f32[4096,256]{1,0:T(8,128)} %v_hbm.1, f32[16,7,256,256]{3,2,1,0:T(8,128)} %blocks.1), custom_call_target="tpu_custom_call" | custom-call | flops 35433480192 | bytes 41943040 | tf_op jit(solution)/shard_map/filter_and_rotate/pallas_call | solution.py:396
  272.6 4.5 %copy.7 = f32[4096,256]{1,0:T(8,128)} copy(f32[4096,256]{1,0:T(8,128)} %filter_and_rotate.1) | data formatting | bytes 8388608
  (1 shorter events, 0.0 us)

commit v3 on v2

--- a/solution.py
+++ b/solution.py
@@ -29,9 +29,9 @@
 def main_kernel(
     n_s, n_b, elem, basis, panel, parts,
     weights, v_hbm, blocks, out,
-    x, xh, xl, fh, fl, wh, wl, f1, recv, g, ar, whole, halo, raw,
+    x, xh, xl, fh, fl, wh, wl, f1, recv, g, ar, whole, halo, raw, dsum, dar, dwhole,
     load_sem, raw_sem, halo_send, halo_recv, a2a_send, a2a_recv, ar_send, ar_recv,
-    z_send, z_recv,
+    z_send, z_recv, d_send, d_recv, dz_send, dz_recv,
     back_send, back_recv, own_sem,
 ):
     s, b = lax.axis_index("space"), lax.axis_index("band")
@@ -175,15 +175,87 @@
             x[rows_of(e)] = filtered_of(e)
             to_home(c, d).start()
         e = b * per_home + c
-        recv[rows_of(e)] = filtered_of(e)
+        value = filtered_of(e)
+        x[rows_of(e)] = value
+        recv[rows_of(e)] = value
         return carry
 
     lax.fori_loop(0, per_home, second_apply, 0)
     for copy in halo2:
         copy.wait_send()
 
-    pairs = [(i, j) for i in range(n_b) for j in range(i, n_b)]
     cuts = panel // LANES
+
+    def partner(bit):
+        return (xor(s, bit), b), lax.rem(s // bit, 2)
+
+    def unpacked(ref, first):
+        return jnp.concatenate(
+            [ref[pl.ds((first + cut) * panel, panel)] for cut in range(cuts)], axis=1)
+
+    dsum[...] = jnp.zeros_like(dsum)
+
+    def add_own(e, carry):
+        value = x[rows_of(e)]
+        product = dot3(split(value.T), split(value))
+        for cut in range(cuts):
+            dsum[pl.ds(cut * panel, panel)] += product[:, cut * LANES:(cut + 1) * LANES]
+        return carry
+
+    lax.fori_loop(0, elem, add_own, 0)
+    own_start, own_half, own_trail, offset = 0, dsum.shape[0], [], 0
+    for k, space_bit in enumerate(space_bits):
+        own_half //= 2
+        target, bit = partner(space_bit)
+        keep = pl.multiple_of(own_start + bit * own_half, 8)
+        give = pl.multiple_of(own_start + (1 - bit) * own_half, 8)
+        copy = pltpu.make_async_remote_copy(
+            src_ref=dsum.at[pl.ds(give, own_half)], dst_ref=dar.at[pl.ds(offset, own_half)],
+            send_sem=d_send.at[0, k], recv_sem=d_recv.at[0, k],
+            device_id=target, device_id_type=MESH)
+        copy.start()
+        copy.wait()
+        dsum[pl.ds(keep, own_half)] += dar[pl.ds(offset, own_half)]
+        own_start = keep
+        own_trail.append((keep, own_half))
+        offset += own_half
+    own_piece = pl.ds(own_start, own_half)
+    dwhole[b, own_piece] = dsum[own_piece]
+    copies = []
+    for d in range(1, n_b):
+        copy = pltpu.make_async_remote_copy(
+            src_ref=dwhole.at[b, own_piece], dst_ref=dwhole.at[b, own_piece],
+            send_sem=dz_send.at[d], recv_sem=dz_recv.at[d],
+            device_id=(s, band_at(d)), device_id_type=MESH)
+        copy.start()
+        copies.append(copy)
+    for copy in copies:
+        copy.wait()
+    for k in reversed(range(len(space_bits))):
+        target, _ = partner(space_bits[k])
+        held = pl.ds(*own_trail[k])
+        copy = pltpu.make_async_remote_copy(
+            src_ref=dwhole.at[:, held], dst_ref=dwhole.at[:, held],
+            send_sem=d_send.at[1, k], recv_sem=d_recv.at[1, k],
+            device_id=target, device_id_type=MESH)
+        copy.start()
+        copy.wait()
+
+    eye = (lax.broadcasted_iota(jnp.int32, (panel, panel), 0)
+           == lax.broadcasted_iota(jnp.int32, (panel, panel), 1))
+    trace = sum(
+        jnp.sum(jnp.where(eye, unpacked(dwhole.at[i], 0), 0.0), keepdims=True)
+        for i in range(n_b))
+    scale = trace / vectors
+
+    def put(i, j, value):
+        columns = slice(j * panel, (j + 1) * panel)
+        wh[i, :panel, columns], wl[i, :panel, columns] = split(value)
+
+    for i in range(n_b):
+        put(i, i, unpacked(dwhole.at[i], 0) / scale)
+
+    pairs = [(i, j) for i in range(n_b) for j in range(i + 1, n_b)]
     g[...] = jnp.zeros_like(g)
 
     def from_home(c, d):
@@ -203,9 +275,9 @@
             high, low = split(recv[at])
             xh[at], xl[at] = high, low
             parts_of.append((high, low))
-        for i in range(n_b):
+        for i in range(n_b - 1):
             turned = split(recv[rows_of(i * per_home + c)].T)
-            for j in range(i, n_b):
+            for j in range(i + 1, n_b):
                 product = dot3(turned, parts_of[j])
                 t = pairs.index((i, j))
                 for cut in range(cuts):
@@ -219,9 +291,6 @@
         space_bits[:1] + (space_bits[1:][::-1] if part % 2 else space_bits[1:])
         for part in range(parts)]
     steps = len(space_bits)
-
-    def partner(bit):
-        return (xor(s, bit), b), lax.rem(s // bit, 2)
 
     starts = [part * length for part in range(parts)]
     trail = []
@@ -295,25 +364,10 @@
         for copy in copies:
             copy.wait()
 
-    def gram_block(t):
-        return jnp.concatenate(
-            [whole[pl.ds((t * cuts + cut) * panel, panel)] for cut in range(cuts)], axis=1)
-
-    eye = (lax.broadcasted_iota(jnp.int32, (panel, panel), 0)
-           == lax.broadcasted_iota(jnp.int32, (panel, panel), 1))
-    trace = sum(
-        jnp.sum(jnp.where(eye, gram_block(pairs.index((i, i))), 0.0), keepdims=True)
-        for i in range(n_b))
-    scale = trace / vectors
-    def put(i, j, value):
-        columns = slice(j * panel, (j + 1) * panel)
-        wh[i, :panel, columns], wl[i, :panel, columns] = split(value)
-
     for t, (i, j) in enumerate(pairs):
-        normed = gram_block(t) / scale
+        normed = unpacked(whole, t * cuts) / scale
         put(i, j, normed)
-        if i != j:
-            put(j, i, normed.T)
+        put(j, i, normed.T)
 
     def polynomial(i):
         high, low = wh[i, :panel, :vectors], wl[i, :panel, :vectors]
@@ -384,7 +438,8 @@
     rows = elem * basis
     per_home = elem // n_b
     devices = n_s * n_b
-    need = n_b * (n_b + 1) // 2 * (panel // LANES) * panel
+    block_rows = panel // LANES * panel
+    need = n_b * (n_b - 1) // 2 * block_rows
     parts = 2 if need % (16 * devices) == 0 else 1
     unit = 8 * devices * parts
     packed = -(-need // unit) * unit
@@ -413,10 +468,14 @@
             pltpu.VMEM((packed, LANES), F32),
             pltpu.VMEM((2, 2, REACH * basis, panel), F32),
             pltpu.VMEM((3, count, basis, basis), F32),
+            pltpu.VMEM((block_rows, LANES), F32),
+            pltpu.VMEM((block_rows, LANES), F32),
+            pltpu.VMEM((n_b, block_rows, LANES), F32),
             dma, dma((3,)), dma((2, 2)), dma((2, 2)),
             dma((per_home, n_b)), dma((per_home, n_b)),
             dma((2, steps, parts)), dma((2, steps, parts)),
             dma((2, n_b, parts)), dma((2, n_b, parts)),
+            dma((2, steps)), dma((2, steps)), dma((n_b,)), dma((n_b,)),
             dma((per_home, n_b)), dma((per_home, n_b)), dma((per_home,)),
         ],
         compiler_params=pltpu.CompilerParams(

time: 278 us -> 286 us (1.029)
  Pallas kernels: 271 us -> 278 us
    pallas_call x1, Pallas kernels: 271 us -> 278 us  [per_device(): pl.pallas_call(functools.partial(main_kernel, n_s, n_b, elem, basis, pane...]
where the time goes in v3:
time: 286 us; the launch traced here: 285 us
  Pallas kernels  278 us (97%)
  local copies, waits for them, and re-layouts  5.33 us (2%)
    pallas_call x1, Pallas kernels, per_device(): pl.pallas_call(functools.partial(main_kernel, n_s, n_b, elem, basis, pane...  278 us

profile of v3, /device:TPU:9, one launch (start us, length us, event | category | flops | bytes accessed | tf_op | source)
XLA Modules:
  0.0 284.6 jit_solution(846192107871102785)
XLA Ops:
  0.0 0.7 add_select_fusion
  0.7 0.1 copy.5
  0.8 0.1 fusion
  0.9 0.8 reshape.11.weights
  1.7 278.4 %filter_and_rotate.1 = f32[4096,256]{1,0:T(8,128)} custom-call(f32[560]{0:T(1024)} %reshape.11.weights, f32[4096,256]{1,0:T(8,128)} %v_hbm.1, f32[16,7,256,256]{3,2,1,0:T(8,128)} %blocks.1), custom_call_target="tpu_custom_call" | custom-call | flops 35433480192 | bytes 41943040 | tf_op jit(solution)/shard_map/filter_and_rotate/pallas_call | solution.py:451
  280.1 4.5 %copy.7 = f32[4096,256]{1,0:T(8,128)} copy(f32[4096,256]{1,0:T(8,128)} %filter_and_rotate.1) | data formatting | bytes 8388608
  (1 shorter events, 0.0 us)

commit v4 on v2

--- a/solution.py
+++ b/solution.py
@@ -29,9 +29,9 @@
 def main_kernel(
     n_s, n_b, elem, basis, panel, parts,
     weights, v_hbm, blocks, out,
-    x, xh, xl, fh, fl, wh, wl, f1, recv, g, ar, whole, halo, raw,
+    x, xh, xl, fh, fl, wh, wl, f1, recv, g, ar, whole, halo, raw, dsum, dar, dwhole,
     load_sem, raw_sem, halo_send, halo_recv, a2a_send, a2a_recv, ar_send, ar_recv,
-    z_send, z_recv,
+    z_send, z_recv, d_send, d_recv, dz_send, dz_recv,
     back_send, back_recv, own_sem,
 ):
     s, b = lax.axis_index("space"), lax.axis_index("band")
@@ -173,17 +173,35 @@
         for d in far_first:
             e = band_at(d) * per_home + c
             x[rows_of(e)] = filtered_of(e)
-            to_home(c, d).start()
+            if carry:
+                to_home(c, d).start()
         e = b * per_home + c
-        recv[rows_of(e)] = filtered_of(e)
-        return carry
-
-    lax.fori_loop(0, per_home, second_apply, 0)
+        value = filtered_of(e)
+        x[rows_of(e)] = value
+        recv[rows_of(e)] = value
+
+    def send_chunks(first, last):
+        for c in range(first, last):
+            for d in far_first:
+                to_home(c, d).start()
+
+    early = per_home // 2
+    middle = early + (per_home - early) // 2
+    pl.loop(0, early)(lambda c: second_apply(c, True))
+    pl.loop(early, per_home)(lambda c: second_apply(c, False))
     for copy in halo2:
         copy.wait_send()
 
-    pairs = [(i, j) for i in range(n_b) for j in range(i, n_b)]
     cuts = panel // LANES
+
+    def partner(bit):
+        return (xor(s, bit), b), lax.rem(s // bit, 2)
+
+    def unpacked(ref, first):
+        return jnp.concatenate(
+            [ref[pl.ds((first + cut) * panel, panel)] for cut in range(cuts)], axis=1)
+
+    pairs = [(i, j) for i in range(n_b) for j in range(i + 1, n_b)]
     g[...] = jnp.zeros_like(g)
 
     def from_home(c, d):
@@ -203,16 +221,58 @@
             high, low = split(recv[at])
             xh[at], xl[at] = high, low
             parts_of.append((high, low))
-        for i in range(n_b):
+        for i in range(n_b - 1):
             turned = split(recv[rows_of(i * per_home + c)].T)
-            for j in range(i, n_b):
+            for j in range(i + 1, n_b):
                 product = dot3(turned, parts_of[j])
                 t = pairs.index((i, j))
                 for cut in range(cuts):
                     g[pl.ds((t * cuts + cut) * panel, panel)] += product[:, cut * LANES:(cut + 1) * LANES]
         return carry
 
-    lax.fori_loop(0, per_home, add_gram, 0)
+    dsum[...] = jnp.zeros_like(dsum)
+
+    def add_own(e, carry):
+        value = x[rows_of(e)]
+        product = dot3(split(value.T), split(value))
+        for cut in range(cuts):
+            dsum[pl.ds(cut * panel, panel)] += product[:, cut * LANES:(cut + 1) * LANES]
+        return carry
+
+    lax.fori_loop(0, elem, add_own, 0)
+    own_start, own_half, own_trail, offset = 0, dsum.shape[0], [], 0
+    for k, space_bit in enumerate(space_bits):
+        own_half //= 2
+        target, bit = partner(space_bit)
+        keep = pl.multiple_of(own_start + bit * own_half, 8)
+        give = pl.multiple_of(own_start + (1 - bit) * own_half, 8)
+        copy = pltpu.make_async_remote_copy(
+            src_ref=dsum.at[pl.ds(give, own_half)], dst_ref=dar.at[pl.ds(offset, own_half)],
+            send_sem=d_send.at[0, k], recv_sem=d_recv.at[0, k],
+            device_id=target, device_id_type=MESH)
+        copy.start()
+        if k == 0:
+            send_chunks(early, middle)
+        if k == 1:
+            send_chunks(middle, per_home)
+        if k == len(space_bits) - 1:
+            lax.fori_loop(0, per_home - 1, add_gram, 0)
+        copy.wait()
+        dsum[pl.ds(keep, own_half)] += dar[pl.ds(offset, own_half)]
+        own_start = keep
+        own_trail.append((keep, own_half))
+        offset += own_half
+    own_piece = pl.ds(own_start, own_half)
+    dwhole[b, own_piece] = dsum[own_piece]
+    own_copies = []
+    for d in range(1, n_b):
+        copy = pltpu.make_async_remote_copy(
+            src_ref=dwhole.at[b, own_piece], dst_ref=dwhole.at[b, own_piece],
+            send_sem=dz_send.at[d], recv_sem=dz_recv.at[d],
+            device_id=(s, band_at(d)), device_id_type=MESH)
+        copy.start()
+        own_copies.append(copy)
+    add_gram(per_home - 1, 0)
 
     length = g.shape[0] // parts
     orders = [
@@ -220,32 +280,37 @@
         for part in range(parts)]
     steps = len(space_bits)
 
-    def partner(bit):
-        return (xor(s, bit), b), lax.rem(s // bit, 2)
-
     starts = [part * length for part in range(parts)]
     trail = []
     offset = 0
+
+    def halve(part, k, offset):
+        half = length >> (k + 1)
+        target, bit = partner(orders[part][k])
+        keep = pl.multiple_of(starts[part] + bit * half, 8)
+        give = pl.multiple_of(starts[part] + (1 - bit) * half, 8)
+        copy = pltpu.make_async_remote_copy(
+            src_ref=g.at[pl.ds(give, half)], dst_ref=ar.at[part, pl.ds(offset, half)],
+            send_sem=ar_send.at[0, k, part], recv_sem=ar_recv.at[0, k, part],
+            device_id=target, device_id_type=MESH)
+        copy.start()
+        return copy, keep
+
+    current = [halve(part, 0, 0) for part in range(parts)]
+    halved = []
     for k in range(steps):
         half = length >> (k + 1)
-        copies, keeps = [], []
-        for part in range(parts):
-            target, bit = partner(orders[part][k])
-            keep = pl.multiple_of(starts[part] + bit * half, 8)
-            give = pl.multiple_of(starts[part] + (1 - bit) * half, 8)
-            copy = pltpu.make_async_remote_copy(
-                src_ref=g.at[pl.ds(give, half)], dst_ref=ar.at[part, pl.ds(offset, half)],
-                send_sem=ar_send.at[0, k, part], recv_sem=ar_recv.at[0, k, part],
-                device_id=target, device_id_type=MESH)
-            copy.start()
-            copies.append(copy)
-            keeps.append(keep)
-        for part in range(parts):
-            copies[part].wait()
-            g[pl.ds(keeps[part], half)] += ar[part, pl.ds(offset, half)]
-            starts[part] = keeps[part]
-        trail.append(keeps)
+        trail.append([keep for _, keep in current])
+        for part, (copy, keep) in enumerate(current):
+            copy.wait_recv()
+            halved.append(copy)
+            g[pl.ds(keep, half)] += ar[part, pl.ds(offset, half)]
+            starts[part] = keep
+            if k + 1 < steps:
+                current[part] = halve(part, k + 1, offset + half)
         offset += half
+    for copy in halved:
+        copy.wait_send()
     piece = (length >> steps) // n_b
 
     def piece_at(part, index):
@@ -278,11 +343,18 @@
                 device_id=(s, band_at(d)), device_id_type=MESH)
             copy.start()
             copies.append(copy)
-    for copy in copies:
+    for copy in copies + own_copies:
         copy.wait()
     for k in reversed(range(steps)):
         half = length >> (k + 1)
-        copies = []
+        target, _ = partner(space_bits[k])
+        held = pl.ds(*own_trail[k])
+        copy = pltpu.make_async_remote_copy(
+            src_ref=dwhole.at[:, held], dst_ref=dwhole.at[:, held],
+            send_sem=d_send.at[1, k], recv_sem=d_recv.at[1, k],
+            device_id=target, device_id_type=MESH)
+        copy.start()
+        copies = [copy]
         for part in range(parts):
             target, _ = partner(orders[part][k])
             keep = trail[k][part]
@@ -295,25 +367,24 @@
         for copy in copies:
             copy.wait()
 
-    def gram_block(t):
-        return jnp.concatenate(
-            [whole[pl.ds((t * cuts + cut) * panel, panel)] for cut in range(cuts)], axis=1)
-
     eye = (lax.broadcasted_iota(jnp.int32, (panel, panel), 0)
            == lax.broadcasted_iota(jnp.int32, (panel, panel), 1))
     trace = sum(
-        jnp.sum(jnp.where(eye, gram_block(pairs.index((i, i))), 0.0), keepdims=True)
+        jnp.sum(jnp.where(eye, unpacked(dwhole.at[i], 0), 0.0), keepdims=True)
         for i in range(n_b))
     scale = trace / vectors
+
     def put(i, j, value):
         columns = slice(j * panel, (j + 1) * panel)
         wh[i, :panel, columns], wl[i, :panel, columns] = split(value)
 
+    for i in range(n_b):
+        put(i, i, unpacked(dwhole.at[i], 0) / scale)
+
     for t, (i, j) in enumerate(pairs):
-        normed = gram_block(t) / scale
+        normed = unpacked(whole, t * cuts) / scale
         put(i, j, normed)
-        if i != j:
-            put(j, i, normed.T)
+        put(j, i, normed.T)
 
     def polynomial(i):
         high, low = wh[i, :panel, :vectors], wl[i, :panel, :vectors]
@@ -384,7 +455,8 @@
     rows = elem * basis
     per_home = elem // n_b
     devices = n_s * n_b
-    need = n_b * (n_b + 1) // 2 * (panel // LANES) * panel
+    block_rows = panel // LANES * panel
+    need = n_b * (n_b - 1) // 2 * block_rows
     parts = 2 if need % (16 * devices) == 0 else 1
     unit = 8 * devices * parts
     packed = -(-need // unit) * unit
@@ -413,10 +485,14 @@
             pltpu.VMEM((packed, LANES), F32),
             pltpu.VMEM((2, 2, REACH * basis, panel), F32),
             pltpu.VMEM((3, count, basis, basis), F32),
+            pltpu.VMEM((block_rows, LANES), F32),
+            pltpu.VMEM((block_rows, LANES), F32),
+            pltpu.VMEM((n_b, block_rows, LANES), F32),
             dma, dma((3,)), dma((2, 2)), dma((2, 2)),
             dma((per_home, n_b)), dma((per_home, n_b)),
             dma((2, steps, parts)), dma((2, steps, parts)),
             dma((2, n_b, parts)), dma((2, n_b, parts)),
+            dma((2, steps)), dma((2, steps)), dma((n_b,)), dma((n_b,)),
             dma((per_home, n_b)), dma((per_home, n_b)), dma((per_home,)),
         ],
         compiler_params=pltpu.CompilerParams(

time: 278 us -> 274 us (0.986)
  Pallas kernels: 271 us -> 267 us
    pallas_call x1, Pallas kernels: 271 us -> 267 us  [per_device(): pl.pallas_call(functools.partial(main_kernel, n_s, n_b, elem, basis, pane...]
where the time goes in v4:
time: 274 us
  Pallas kernels  267 us (97%)
  local copies, waits for them, and re-layouts  5.33 us (2%)
    pallas_call x1, Pallas kernels, per_device(): pl.pallas_call(functools.partial(main_kernel, n_s, n_b, elem, basis, pane...  267 us

profile of v4, /device:TPU:9, one launch (start us, length us, event | category | flops | bytes accessed | tf_op | source)
XLA Modules:
  0.0 273.6 jit_solution(15197382950132432001)
XLA Ops:
  0.0 0.7 add_select_fusion
  0.7 0.1 copy.5
  0.8 0.1 fusion
  0.9 0.8 reshape.11.weights
  1.7 267.5 %filter_and_rotate.1 = f32[4096,256]{1,0:T(8,128)} custom-call(f32[560]{0:T(1024)} %reshape.11.weights, f32[4096,256]{1,0:T(8,128)} %v_hbm.1, f32[16,7,256,256]{3,2,1,0:T(8,128)} %blocks.1), custom_call_target="tpu_custom_call" | custom-call | flops 35433480192 | bytes 41943040 | tf_op jit(solution)/shard_map/filter_and_rotate/pallas_call | solution.py:468
  269.2 4.5 %copy.7 = f32[4096,256]{1,0:T(8,128)} copy(f32[4096,256]{1,0:T(8,128)} %filter_and_rotate.1) | data formatting | bytes 8388608
  (1 shorter events, 0.0 us)
